TPU v7x, 32 devices: a whole 2x2x4 slice. The times are simulated.
32 devices in a mesh: row: 8 (over z, y), col: 4 (over x, core).
Axes of the slice: x: 2, y: 2, z: 4, core: 2. Of those that a mesh axis runs over, the one named last changes fastest.
Arguments:
- a_weights: bfloat16 [4096, 1024], P('row', 'col'), may hold values from 0.0001 to 1, as said below
- tile_mask: int32 [8, 2], replicated, may hold values from 0 to 1, as said below
- pair_mask: int32 [8, 8], replicated, may hold values from 0 to 1, as said below
Outputs:
- jaccard: bfloat16 [4096, 4096], P('row', 'col')
Inputs may be any that keep to these rules, and one draw needn't show every extreme that they name: `a_weights`: all weights positive. `tile_mask`: 1 where a tile is present; tile (I, I mod 2) of every block row I is present. `pair_mask`: symmetric, with ones on the diagonal.
All inputs are finite; a program needn't handle non-finite values.
Results may differ from a plain program's by a relative error of at most 0.001.
Values may be sent and summed in bfloat16 or wider, within the bound.
A program may use at most 64 MiB of HBM per device.

v0:
```python
import jax
import jax.numpy as jnp
from jax import lax
from jax.sharding import PartitionSpec as P

BLOCK = 512


def broadcast(value, axis, source):
    kept = jnp.where(lax.axis_index(axis) == source, value, 0).astype(value.dtype)
    return lax.psum(kept, axis)


def expand_tiles(flags):
    return jnp.repeat(jnp.repeat(flags, BLOCK, axis=0), BLOCK, axis=1)


def body(a_weights, tile_mask, pair_mask):
    row_index = lax.axis_index("row")
    col_index = lax.axis_index("col")
    pair_count = lax.axis_size("row") // lax.axis_size("col")
    blocks_here = a_weights.shape[0] // BLOCK
    own_flags = lax.dynamic_slice_in_dim(tile_mask, row_index * blocks_here, blocks_here, 0)
    own_mask = expand_tiles(own_flags).astype(jnp.bfloat16)
    gathered = lax.all_gather(a_weights, "col", axis=1, tiled=True)
    own_panel = gathered * own_mask
    row_degree = jnp.einsum("ik,ik->i", own_panel, own_panel, preferred_element_type=jnp.float32)
    remotes = [
        broadcast(own_panel, "row", pair_count * col_index + offset) for offset in range(pair_count)
    ]
    outputs = []
    for offset in range(pair_count):
        col_first = (pair_count * col_index + offset) * blocks_here
        remote = remotes[offset]
        pair_tiles = lax.dynamic_slice(
            pair_mask, (row_index * blocks_here, col_first), (blocks_here, blocks_here)
        )
        pair_open = expand_tiles(pair_tiles) > 0
        col_degree = jnp.einsum("ik,ik->i", remote, remote, preferred_element_type=jnp.float32)
        shared = lax.dot_general(
            own_panel, remote, (((1,), (1,)), ((), ())), preferred_element_type=jnp.float32
        )
        weights = shared / (row_degree[:, None] + col_degree[None, :] - shared)
        outputs.append(jnp.where(pair_open, weights, jnp.zeros_like(weights)))
    return jnp.concatenate(outputs, axis=1).astype(jnp.bfloat16)


def solution(mesh):
    in_specs = (P("row", "col"), P(), P())
    out_specs = P("row", "col")
    return jax.shard_map(body, mesh=mesh, in_specs=in_specs, out_specs=out_specs, check_vma=False)
```

profile of v0, /device:TPU:3, one launch (start us, length us, event | category | flops | bytes accessed | tf_op | source)
XLA Modules:
  0.0 145.1 jit_solution(6093091236768662315)
XLA Ops:
  6.5 0.0 all-gather.2.cloned.1.call-start
  6.5 0.7 all-gather.2.cloned.1.call-update
  7.3 0.0 all-reduce.3.cloned.1.call-start
  7.3 0.9 fusion.17
  8.2 0.1 broadcast_bitcast_fusion
  8.3 18.0 %all-gather.2.cloned.1.call-done = bf16[512,1024]{1,0:T(8,128)(2,1)} async-done(((bf16[512,256]{1,0:T(8,128)(2,1)}), bf16[512,1024]{1,0:T(8,128)(2,1)}) %all-gather.2.cloned.1.call-update) | async-done | bytes 1048592 | tf_op jit(solution)/shard_map/all_gather | solution.py:25
  26.3 2.7 %broadcast_select_fusion.1 = (bf16[512,1024]{1,0:T(8,128)(2,1)}, bf16[512,1024]{1,0:T(8,128)(2,1)}) fusion(pred[]{:T(512)S(6)} %eq.6, bf16[512,1024]{1,0:T(8,128)(2,1)} %all-gather.2.cloned.1.call-done, bf16[1024]{0:T(1024)(128)(2,1)S(1)} %bitcast.7, pred[]{:T(512)S(6)} %eq.7), kind=kLoop, calls=%fused_computation.14 | loop fusion | flops 1572864 | bytes 3147778 | tf_op jit(solution)/shard_map/jit(_where)/select_n | solution.py:10
  29.0 0.0 copy-start
  29.0 0.0 all-reduce.3.cloned.1.call-update
  29.0 1.5 %fusion.18 = (s32[1,1]{1,0:T(1,128)}, s32[1,1]{1,0:T(1,128)}) fusion(s32[8,8]{1,0:T(8,128)} %param.5, s32[]{:T(128)S(6)} %select_n.32, s32[]{:T(128)S(6)} %select_n.33, s32[]{:T(128)S(6)} %select_n.37), kind=kLoop, calls=%fused_computation.24 | loop fusion | bytes 28 | tf_op jit(solution)/shard_map/dynamic_slice | solution.py:35
  31.8 0.0 copy-done
  31.8 0.3 fusion.2
  32.1 100.5 %all-reduce.3.cloned.1.call-done = (bf16[512,1024]{1,0:T(8,128)(2,1)}, bf16[512,1024]{1,0:T(8,128)(2,1)}) async-done(((bf16[512,1024]{1,0:T(8,128)(2,1)}, bf16[512,1024]{1,0:T(8,128)(2,1)}), (bf16[512,1024]{1,0:T(8,128)(2,1)}, bf16[512,1024]{1,0:T(8,128)(2,1)})) %all-reduce.3.cloned.1.call-update) | async-done | bytes 2097168 | tf_op jit(solution)/shard_map/psum | solution.py:11
  132.7 0.0 copy-start.2
  132.7 2.1 %fusion = (f32[512]{0:T(512)S(1)}, f32[512]{0:T(512)S(1)}) fusion(bf16[512,1024]{1,0:T(8,128)(2,1)} %get-tuple-element.5, bf16[512,1024]{1,0:T(8,128)(2,1)} %get-tuple-element.6), kind=kLoop, calls=%fused_computation.1 | loop fusion | flops 3144704 | bytes 2101248 | tf_op jit(solution)/shard_map/ik,ik->i/dot_general | solution.py:39
  134.8 0.0 copy-done.2
  134.8 0.0 copy-start.1
  134.8 0.8 fusion.4
  135.6 0.4 copy-done.1
  136.0 0.8 fusion.6
  136.8 0.1 pad_maximum_fusion
  136.9 1.3 copy.4
  (1 shorter events, 0.0 us)
Async XLA Ops:
  6.5 19.7 %all-gather.2.cloned.1.call-start = ((), (), s32[]{:S(2)}) async-start(), calls=%async_computation | async-start | bytes 1310720 | tf_op jit(solution)/shard_map/all_gather | solution.py:25
  7.3 125.4 %all-reduce.3.cloned.1.call-start = ((), (), s32[]{:S(2)}) async-start(), calls=%async_computation.1 | async-start | bytes 4194304 | tf_op jit(solution)/shard_map/psum | solution.py:11
  29.0 2.8 %copy-start = (bf16[512,1024]{1,0:T(8,128)(2,1)S(1)}, bf16[512,1024]{1,0:T(8,128)(2,1)}, u32[]{:S(2)}) copy-start(bf16[512,1024]{1,0:T(8,128)(2,1)} %all-gather.2.cloned.1.call-done) | copy-start | bytes 3145732
  132.7 2.1 %copy-start.2 = (bf16[512,1024]{1,0:T(8,128)(2,1)S(1)}, bf16[512,1024]{1,0:T(8,128)(2,1)}, u32[]{:S(2)}) copy-start(bf16[512,1024]{1,0:T(8,128)(2,1)} %get-tuple-element.6) | copy-start | bytes 3145732
  134.8 1.2 copy-start.1
Sparse Core Ops, SparseCore 0:
  8.9 17.3 all-gather.1
  29.9 102.6 all-reduce.2
where the time goes:
time: 147 us; the launch traced here: 145 us
  waiting for transfers between devices  119 us (81%)
  between operations  14.8 us (10%)
  other arithmetic  6.09 us (4%)
  local copies, waits for them, and re-layouts  3.29 us (2%)
  matrix products  1.58 us (1%)
    psum x1, waiting for transfers between devices, broadcast(): return lax.psum(kept, axis)  101 us
    all_gather x1, waiting for transfers between devices, body(): gathered = lax.all_gather(a_weights, 'col', axis=1, tiled=True)  18 us
  transfers between devices with their start and end apart: 2, of which 2 were waited for; matrix products, arithmetic and copies ran while one was open for 2% of the time, Pallas kernels for 0%

commit v1 on v0

v1 whole, which is shorter than its diff:
```python
import functools

import jax
import jax.numpy as jnp
from jax import lax
from jax.experimental import pallas as pl
from jax.experimental.pallas import tpu as pltpu
from jax.sharding import PartitionSpec as P

BLOCK = 512
PIECES = 2
MESH = pl.DeviceIdType.MESH
UP, DOWN, SIDE, CORE = range(4)


def kernel(rows, cols, tile_ref, pair_ref, a_ref, out_ref, buf, send_x, send, recv):
    levels, chips = rows // 2, cols // 2
    width = a_ref.shape[1]
    part = BLOCK // PIECES
    row, col = lax.axis_index("row"), lax.axis_index("col")
    z, y = row // 2, row % 2
    q, k = col // 2, col % 2
    near = z // 2 == q
    slot = jnp.where(near, 2 * (z - 2 * q) + y, 4)

    flag = tile_ref[row, (col * width) // BLOCK]
    own = a_ref[...]
    buf[slot, col] = jnp.where(flag > 0, own, jnp.zeros_like(own))

    up_id, down_id = (row + 2, col), (row - 2, col)
    side_id, core_id = (row + 1 - 2 * y, col), (row, col + 1 - 2 * k)
    x_ids = [(row, lax.rem(col + 2 * i, cols)) for i in range(1, chips)]
    has_up, has_down = z + 1 < levels, z > 0

    barrier = pltpu.get_barrier_semaphore()
    for device in [side_id, core_id] + x_ids:
        pl.semaphore_signal(barrier, inc=1, device_id=device, device_id_type=MESH)
    for there, device in ((has_up, up_id), (has_down, down_id)):

        @pl.when(there)
        def _():
            pl.semaphore_signal(barrier, inc=1, device_id=device, device_id_type=MESH)

    pl.semaphore_wait(
        barrier, chips + 1 + has_up.astype(jnp.int32) + has_down.astype(jnp.int32)
    )

    sent = []

    def copy(kind, j, s, p, device):
        ref = buf.at[j, 2 * s + k, pl.ds(p * part, part), :]
        return pltpu.make_async_remote_copy(
            src_ref=ref, dst_ref=ref, send_sem=send.at[kind, j, s, p],
            recv_sem=recv.at[j, 2 * s + k, p], device_id=device, device_id_type=MESH)

    def start(when, kind, j, s, p, device):
        made = copy(kind, j, s, p, device)
        sent.append((when, made))
        if when is None:
            made.start()
        else:
            pl.when(when)(made.start)

    def arrived(j, s, parity, p):
        ref = buf.at[j, 2 * s + parity, pl.ds(p * part, part), :]
        pltpu.make_async_remote_copy(
            src_ref=ref, dst_ref=ref, send_sem=send.at[CORE, j, s, p],
            recv_sem=recv.at[j, 2 * s + parity, p], device_id=core_id,
            device_id_type=MESH).wait_recv()

    for p in range(PIECES):
        for i, device in enumerate(x_ids):
            other = device[1] // 2
            there = jnp.where(z // 2 == other, 2 * (z - 2 * other) + y, 4)
            made = pltpu.make_async_remote_copy(
                src_ref=buf.at[slot, col, pl.ds(p * part, part), :],
                dst_ref=buf.at[there, col, pl.ds(p * part, part), :],
                send_sem=send_x.at[i, p], recv_sem=recv.at[there, col, p],
                device_id=device, device_id_type=MESH)
            sent.append((None, made))
            made.start()

    def from_side(a, s, p):
        j = 2 * a + 1 - y
        arrived(j, s, k, p)
        start(a == 1 - k, CORE, j, s, p, core_id)

    far_first = (z > 2 * q).astype(jnp.int32)
    items = [
        (far_first if a == 0 else 1 - far_first, i, p)
        for a in range(2) for i in range(chips) for p in range(PIECES)
    ]
    before = []
    for a, i, p in items:
        s = lax.rem(q + i, chips)
        j = 2 * a + y
        here = z == 2 * q + a
        if i == 0:
            pl.when(jnp.logical_not(here))(functools.partial(arrived, j, s, k, p))
        else:
            arrived(j, s, k, p)
        start(has_up & (z >= 2 * q + a), UP, j, s, p, up_id)
        start(has_down & (z <= 2 * q + a), DOWN, j, s, p, down_id)
        start(None, SIDE, j, s, p, side_id)
        start(here | (a == 1 - k), CORE, j, s, p, core_id)
        before.append((a, s, p))
        if len(before) > 2:
            from_side(*before.pop(0))
    for args in before:
        from_side(*args)

    far = jnp.logical_not(near)
    for i in range(chips):
        for p in range(PIECES):
            s = lax.rem(q + i, chips)
            if i > 0:
                pl.when(far)(functools.partial(arrived, 4, s, k, p))
            start(far, CORE, 4, s, p, core_id)
    for s in range(chips):
        for p in range(PIECES):
            arrived(slot, s, 1 - k, p)
            for other in range(2):
                j = 2 * k + other
                pl.when(j != slot)(functools.partial(arrived, j, s, 1 - k, p))

    ones = jnp.ones((8, width), jnp.bfloat16)
    dims = (((1,), (1,)), ((), ()))
    row_degree = jnp.zeros((BLOCK, 1), jnp.float32)
    for s in range(cols):
        mine = buf[slot, s].astype(jnp.float32)
        row_degree += jnp.sum(mine * mine, axis=1, keepdims=True)
    for other in range(2):
        j = 2 * k + other
        open_pair = pair_ref[row, 2 * col + other] > 0
        for p in range(PIECES):
            shared = jnp.zeros((BLOCK, part), jnp.float32)
            degree = jnp.zeros((8, part), jnp.float32)
            for s in range(cols):
                theirs = buf[j, s, p * part:(p + 1) * part, :]
                shared += lax.dot_general(
                    buf[slot, s], theirs, dims, preferred_element_type=jnp.float32)
                wide = theirs.astype(jnp.float32)
                square = wide * wide
                high = square.astype(jnp.bfloat16)
                low = (square - high.astype(jnp.float32)).astype(jnp.bfloat16)
                degree += lax.dot_general(ones, high, dims, preferred_element_type=jnp.float32)
                degree += lax.dot_general(ones, low, dims, preferred_element_type=jnp.float32)
            weights = shared / (row_degree + degree[:1] - shared)
            weights = jnp.where(open_pair, weights, jnp.zeros_like(weights))
            first = other * BLOCK + p * part
            out_ref[:, first:first + part] = weights.astype(jnp.bfloat16)

    for when, made in sent:
        if when is None:
            made.wait_send()
        else:
            pl.when(when)(made.wait_send)


def body(rows, cols, a_weights, tile_mask, pair_mask):
    width = a_weights.shape[1]
    chips = cols // 2
    return pl.pallas_call(
        functools.partial(kernel, rows, cols),
        out_shape=jax.ShapeDtypeStruct((BLOCK, rows // cols * BLOCK), jnp.bfloat16),
        in_specs=[
            pl.BlockSpec(memory_space=pltpu.SMEM),
            pl.BlockSpec(memory_space=pltpu.SMEM),
            pl.BlockSpec(memory_space=pltpu.VMEM),
        ],
        out_specs=pl.BlockSpec(memory_space=pltpu.VMEM),
        scratch_shapes=[
            pltpu.VMEM((5, cols, BLOCK, width), jnp.bfloat16),
            pltpu.SemaphoreType.DMA((chips - 1, PIECES)),
            pltpu.SemaphoreType.DMA((4, 5, chips, PIECES)),
            pltpu.SemaphoreType.DMA((5, cols, PIECES)),
        ],
        compiler_params=pltpu.CompilerParams(
            collective_id=0, has_side_effects=True, vmem_limit_bytes=40 * 2**20),
        cost_estimate=pl.CostEstimate(
            flops=4 * BLOCK * BLOCK * width * cols, bytes_accessed=4 * BLOCK * BLOCK,
            transcendentals=0),
    )(tile_mask, pair_mask, a_weights)


def solution(mesh):
    rows, cols = mesh.shape["row"], mesh.shape["col"]
    in_specs = (P("row", "col"), P(), P())
    out_specs = P("row", "col")
    return jax.shard_map(
        functools.partial(body, rows, cols), mesh=mesh, in_specs=in_specs,
        out_specs=out_specs, check_vma=False)
```

time: 147 us -> 46.5 us (0.32); the launches traced: 145 us -> 46.4 us
  waiting for transfers between devices: 119 us -> 0 us
  Pallas kernels: 0 us -> 43.7 us
  between operations: 14.8 us -> 0.01 us
  other arithmetic: 6.09 us -> 0 us
  matrix products: 1.58 us -> 0 us
    psum x1 -> x0, waiting for transfers between devices: 101 us -> none  [broadcast(): return lax.psum(kept, axis)]
    pallas_call x0 -> x1, Pallas kernels: none -> 43.7 us  [body(): pl.pallas_call(functools.partial(kernel, rows, cols), out_shape=jax.Shape...]
    all_gather x1 -> x0, waiting for transfers between devices: 18 us -> none  [body(): gathered = lax.all_gather(a_weights, 'col', axis=1, tiled=True)]
    select_n x1 -> x0, other arithmetic: 2.69 us -> none  [broadcast(): jnp.where(lax.axis_index(axis) == source, value, 0).astype(value.dtype)]
    dot_general x2 -> x0, other arithmetic: 2.46 us -> none  [the longest x1 2.11 us: body(): jnp.einsum('ik,ik->i', remote, remote, preferred_element_type=jnp.float32)]
    unnamed x8 -> x6, local copies, waits for them, and re-layouts: 0.51 us -> 2.69 us
    dot_general x2 -> x0, matrix products: 1.58 us -> none  [body(): lax.dot_general(own_panel, remote, (((1,), (1,)), ((), ())), preferred_el...]
  transfers between devices with their start and end apart: 2 -> 0, of which waited for: 2 -> 0; matrix products, arithmetic and copies ran while one was open for 2% -> 0% of each run, Pallas kernels for 0% -> 0%
where the time goes in v1:
time: 46.5 us; the launch traced here: 46.4 us
  Pallas kernels  43.7 us (94%)
  local copies, waits for them, and re-layouts  2.69 us (6%)
    pallas_call x1, Pallas kernels, body(): pl.pallas_call(functools.partial(kernel, rows, cols), out_shape=jax.Shape...  43.7 us
    unnamed x6, local copies, waits for them, and re-layouts  2.69 us

profile of v1, /device:TPU:3, one launch (start us, length us, event | category | flops | bytes accessed | tf_op | source)
XLA Modules:
  0.0 46.4 jit_solution(416178497891154005)
XLA Ops:
  0.0 0.0 copy-start.1
  0.0 0.8 %copy.4.tile_ref = s32[8,2]{1,0:T(8,128)S(1)} copy(s32[8,2]{0,1:T(2,128)} %param.4) | data formatting | bytes 128 | tf_op args[1]
  0.8 0.0 copy-done.1
  0.8 0.0 copy-start
  0.8 0.9 %copy-done = bf16[512,256]{1,0:T(8,128)(2,1)S(1)} copy-done((bf16[512,256]{1,0:T(8,128)(2,1)S(1)}, bf16[512,256]{1,0:T(8,128)(2,1)}, u32[]{:S(2)}) %copy-start) | copy-done | bytes 262168
  1.7 43.7 %shard_map.37 = bf16[512,1024]{1,0:T(8,128)(2,1)S(1)} custom-call(s32[8,2]{1,0:T(8,128)S(1)} %copy.4.tile_ref, s32[8,8]{1,0:T(8,128)S(1)} %copy-done.1, bf16[512,256]{1,0:T(8,128)(2,1)S(1)} %copy-done), custom_call_target="tpu_custom_call" | custom-call | flops 1073741824 | bytes 1048576 | tf_op jit(solution)/shard_map/pallas_call | solution.py:163
  45.4 1.0 %copy.6 = bf16[512,1024]{1,0:T(8,128)(2,1)} copy(bf16[512,1024]{1,0:T(8,128)(2,1)S(1)} %shard_map.37) | data formatting | bytes 2097152
Async XLA Ops:
  0.0 0.8 %copy-start.1 = (s32[8,8]{1,0:T(8,128)S(1)}, s32[8,8]{1,0:T(8,128)}, u32[]{:S(2)}) copy-start(s32[8,8]{1,0:T(8,128)} %pair_ref.1) | copy-start | bytes 772
  0.8 1.0 %copy-start = (bf16[512,256]{1,0:T(8,128)(2,1)S(1)}, bf16[512,256]{1,0:T(8,128)(2,1)}, u32[]{:S(2)}) copy-start(bf16[512,256]{1,0:T(8,128)(2,1)} %a_ref.1) | copy-start | bytes 786436

commit v2 on v1

--- a/solution.py
+++ b/solution.py
@@ -8,7 +8,8 @@
 from jax.sharding import PartitionSpec as P
 
 BLOCK = 512
-PIECES = 2
+PIECES = 4
+LAG = 4
 MESH = pl.DeviceIdType.MESH
 UP, DOWN, SIDE, CORE = range(4)
 
@@ -104,10 +105,8 @@
         start(None, SIDE, j, s, p, side_id)
         start(here | (a == 1 - k), CORE, j, s, p, core_id)
         before.append((a, s, p))
-        if len(before) > 2:
+        if len(before) > LAG:
             from_side(*before.pop(0))
-    for args in before:
-        from_side(*args)
 
     far = jnp.logical_not(near)
     for i in range(chips):
@@ -119,9 +118,6 @@
     for s in range(chips):
         for p in range(PIECES):
             arrived(slot, s, 1 - k, p)
-            for other in range(2):
-                j = 2 * k + other
-                pl.when(j != slot)(functools.partial(arrived, j, s, 1 - k, p))
 
     ones = jnp.ones((8, width), jnp.bfloat16)
     dims = (((1,), (1,)), ((), ()))
@@ -129,14 +125,26 @@
     for s in range(cols):
         mine = buf[slot, s].astype(jnp.float32)
         row_degree += jnp.sum(mine * mine, axis=1, keepdims=True)
-    for other in range(2):
+    tile = 256
+    for turn in range(2):
+        if turn == 1:
+            for args in before:
+                from_side(*args)
+        other = y if turn == 0 else 1 - y
         j = 2 * k + other
         open_pair = pair_ref[row, 2 * col + other] > 0
-        for p in range(PIECES):
-            shared = jnp.zeros((BLOCK, part), jnp.float32)
-            degree = jnp.zeros((8, part), jnp.float32)
+        for t in range(BLOCK // tile):
+
+            @pl.when(j != slot)
+            def _():
+                for s in range(chips):
+                    for p in range(t * tile // part, (t + 1) * tile // part):
+                        arrived(j, s, 1 - k, p)
+
+            shared = jnp.zeros((BLOCK, tile), jnp.float32)
+            degree = jnp.zeros((8, tile), jnp.float32)
             for s in range(cols):
-                theirs = buf[j, s, p * part:(p + 1) * part, :]
+                theirs = buf[j, s, t * tile:(t + 1) * tile, :]
                 shared += lax.dot_general(
                     buf[slot, s], theirs, dims, preferred_element_type=jnp.float32)
                 wide = theirs.astype(jnp.float32)
@@ -147,8 +155,8 @@
                 degree += lax.dot_general(ones, low, dims, preferred_element_type=jnp.float32)
             weights = shared / (row_degree + degree[:1] - shared)
             weights = jnp.where(open_pair, weights, jnp.zeros_like(weights))
-            first = other * BLOCK + p * part
-            out_ref[:, first:first + part] = weights.astype(jnp.bfloat16)
+            first = pl.multiple_of(other * BLOCK + t * tile, tile)
+            out_ref[:, pl.ds(first, tile)] = weights.astype(jnp.bfloat16)
 
     for when, made in sent:
         if when is None:

time: 46.5 us -> 42.2 us (0.908)
  Pallas kernels: 43.7 us -> 39.3 us
    pallas_call x1, Pallas kernels: 43.7 us -> 39.3 us  [body(): pl.pallas_call(functools.partial(kernel, rows, cols), out_shape=jax.Shape...]
where the time goes in v2:
time: 42.2 us; the launch traced here: 42 us
  Pallas kernels  39.3 us (93%)
  local copies, waits for them, and re-layouts  2.69 us (6%)
    pallas_call x1, Pallas kernels, body(): pl.pallas_call(functools.partial(kernel, rows, cols), out_shape=jax.Shape...  39.3 us
    unnamed x6, local copies, waits for them, and re-layouts  2.69 us

profile of v2, /device:TPU:3, one launch (start us, length us, event | category | flops | bytes accessed | tf_op | source)
XLA Modules:
  0.0 42.0 jit_solution(11906984927629532804)
XLA Ops:
  0.0 0.0 copy-start.1
  0.0 0.8 %copy.4.tile_ref = s32[8,2]{1,0:T(8,128)S(1)} copy(s32[8,2]{0,1:T(2,128)} %param.4) | data formatting | bytes 128 | tf_op args[1]
  0.8 0.0 copy-done.1
  0.8 0.0 copy-start
  0.8 0.9 %copy-done = bf16[512,256]{1,0:T(8,128)(2,1)S(1)} copy-done((bf16[512,256]{1,0:T(8,128)(2,1)S(1)}, bf16[512,256]{1,0:T(8,128)(2,1)}, u32[]{:S(2)}) %copy-start) | copy-done | bytes 262168
  1.7 39.3 %shard_map.37 = bf16[512,1024]{1,0:T(8,128)(2,1)S(1)} custom-call(s32[8,2]{1,0:T(8,128)S(1)} %copy.4.tile_ref, s32[8,8]{1,0:T(8,128)S(1)} %copy-done.1, bf16[512,256]{1,0:T(8,128)(2,1)S(1)} %copy-done), custom_call_target="tpu_custom_call" | custom-call | flops 1073741824 | bytes 1048576 | tf_op jit(solution)/shard_map/pallas_call | solution.py:171
  41.0 1.0 %copy.6 = bf16[512,1024]{1,0:T(8,128)(2,1)} copy(bf16[512,1024]{1,0:T(8,128)(2,1)S(1)} %shard_map.37) | data formatting | bytes 2097152
Async XLA Ops:
  0.0 0.8 %copy-start.1 = (s32[8,8]{1,0:T(8,128)S(1)}, s32[8,8]{1,0:T(8,128)}, u32[]{:S(2)}) copy-start(s32[8,8]{1,0:T(8,128)} %pair_ref.1) | copy-start | bytes 772
  0.8 1.0 %copy-start = (bf16[512,256]{1,0:T(8,128)(2,1)S(1)}, bf16[512,256]{1,0:T(8,128)(2,1)}, u32[]{:S(2)}) copy-start(bf16[512,256]{1,0:T(8,128)(2,1)} %a_ref.1) | copy-start | bytes 786436
